TPU v7x, 512 devices: a whole 4x4x16 slice. The times are simulated.
512 devices in a mesh: dp: 4 (over z_lo), expert: 128 (over y, x, z_hi, core).
Axes of the slice: x: 4, y: 4, z: 16 (z_hi: 4, z_lo: 4; z = z_hi * 4 + z_lo), core: 2. Of those that a mesh axis runs over, the one named last changes fastest.
Arguments:
- hidden_in: bfloat16 [2, 8192, 2048], P(None, ('dp', 'expert')), may hold values from -6 to 6
- cotangent: bfloat16 [2, 8192, 2048], P(None, ('dp', 'expert')), may hold values from -6 to 6
- expert_ids: int32 [2, 8192, 8], P(None, ('dp', 'expert')), may hold values from 0 to 127, all different within a row; in each aligned block of 16 rows (0 to 15, 16 to 31, ..., all dimensions but the last counted through in order) at most 2 rows name the same one
- route_prob: float32 [2, 8192, 8], P(None, ('dp', 'expert')), may hold values from 0.05 to 1
- swap_flags: int32 [64], replicated, may hold values 0 or 1
- gate_up: bfloat16 [128, 2048, 2, 384], P('expert', 'dp'), may hold values from -0.125 to 0.125
- down_t: bfloat16 [128, 2048, 384], P('expert', 'dp'), may hold values from -0.3125 to 0.3125
Outputs:
- hidden_out: bfloat16 [2, 8192, 2048], P(None, ('dp', 'expert'))
- input_grad: bfloat16 [2, 8192, 2048], P(None, ('dp', 'expert'))
- resident_gate_up: bfloat16 [128, 2048, 2, 384], P('expert', 'dp')
- resident_down: bfloat16 [128, 2048, 384], P('expert', 'dp')
Inputs may be any that keep to these rules, and one draw needn't show every extreme that they name: `expert_ids`: within one microbatch the 16 tokens of one device name any one expert at most 2 times, a bound that some block reaches.
All inputs are finite; a program needn't handle non-finite values.
Results may differ from a plain program's by a relative error of at most 0.0064.
Values may be sent and summed in bfloat16 or wider, within the bound.
No kernel may reach another device: no remote copies, remote signals or barrier semaphores. Data moves between devices by JAX's collectives and lax.ppermute only.
A program may use at most 64 MiB of HBM per device.

v0:
```python
import jax
import jax.numpy as jnp
from jax import lax
from jax.sharding import Mesh, PartitionSpec as P

EXPERT = ("y", "x", "z", "c")
PLANE = ("y", "x", "c")
BF = jnp.bfloat16
F32 = jnp.float32


def along_z(value, shift):
    count = lax.axis_size("z")
    return lax.ppermute(value, "z", [(i, (i + shift) % count) for i in range(count)])


def local(hidden_in, cotangent, expert_ids, route_prob, swap_flags, gate_up, down_t):
    micro, tok, width = hidden_in.shape
    top = expert_ids.shape[2]
    hid = down_t.shape[2]
    nz = lax.axis_size("z")
    ny = lax.axis_size("y")
    plane = ny * lax.axis_size("x") * 2
    my_z = lax.axis_index("z")
    my_y = lax.axis_index("y")
    half = ny * lax.axis_size("x") * nz
    my_index = lax.axis_index(EXPERT)
    flag = jnp.sum(jnp.where(jnp.arange(half, dtype=jnp.int32) == my_index % half, swap_flags, 0))
    pairs = [(i, i ^ ny // 2) for i in range(ny)]
    other_gate = lax.ppermute(gate_up, "y", pairs)
    other_down = lax.ppermute(down_t, "y", pairs)
    resident_gate = jnp.where(flag == 1, other_gate, gate_up)
    resident_down = jnp.where(flag == 1, other_down, down_t)
    mine = jnp.stack([hidden_in, cotangent])
    facts = jnp.concatenate([expert_ids.astype(F32), route_prob], axis=2)
    facts = jnp.stack([facts] + [along_z(facts, s) for s in range(1, nz)])
    column = jnp.stack([mine] + [along_z(mine, s) for s in range(1, nz)])
    weights = jnp.concatenate([gate_up.reshape(-1, 2 * hid), down_t.reshape(-1, hid)], axis=1)
    weights = lax.all_gather(weights, "dp", axis=0, tiled=True)
    gate_matrix = weights[:, : 2 * hid]
    down_matrix = weights[:, 2 * hid :]
    ids = facts[..., :top].astype(jnp.int32)
    prob = facts[..., top:]
    core = ids % 2
    place = ids // (2 * nz) * 2 + core
    place = jnp.where(ids // 2 % nz == my_z, place, -1)
    hit = place[..., None] == jnp.arange(plane, dtype=jnp.int32)
    member = jnp.any(hit, axis=3)
    weight = jnp.sum(jnp.where(hit, prob[..., None], 0.0), axis=3)
    below = jnp.tril(jnp.ones((tok, tok), F32), -1)
    earlier = jnp.einsum("ut,smtd->smud", below, member.astype(F32))
    rank = jnp.arange(2, dtype=jnp.int32).astype(F32)
    pick = member[..., None] & (earlier[..., None] == rank)
    pick = pick.astype(F32)
    slot_weight = jnp.einsum("smtdr,smtd->dmsr", pick, weight)
    pick_b = pick.astype(BF)
    rows_x = jnp.einsum(
        "smtdr,smtw->dmsrw", pick_b, column[:, 0], preferred_element_type=F32
    ).astype(BF)
    rows_g = jnp.einsum("smtdr,smtw->dmsrw", pick_b, column[:, 1], preferred_element_type=F32)
    rows_g = (rows_g * slot_weight[..., None]).astype(BF)
    count = micro * nz * 2
    rows = jnp.concatenate(
        [rows_x.reshape(plane, count, width), rows_g.reshape(plane, count, width)], axis=1
    )
    rows = lax.all_to_all(rows, PLANE, 0, 0, tiled=True)
    tokens_now = rows[:, :count].reshape(plane * count, width)
    grads_now = rows[:, count:].reshape(plane * count, width)
    projected = jnp.dot(tokens_now, gate_matrix, preferred_element_type=F32)
    gate_part = projected[:, :hid]
    upper_part = projected[:, hid:]
    sig = jax.nn.sigmoid(gate_part)
    hidden = (gate_part * sig * upper_part).astype(BF)
    last = (((1,), (1,)), ((), ()))
    expert_out = lax.dot_general(hidden, down_matrix, last, preferred_element_type=F32).astype(BF)
    d_hidden = jnp.dot(grads_now, down_matrix, preferred_element_type=F32)
    d_gate = (d_hidden * upper_part * sig * (1.0 + gate_part * (1.0 - sig))).astype(BF)
    d_upper = (d_hidden * gate_part * sig).astype(BF)
    d_joined = jnp.concatenate([d_gate, d_upper], axis=1)
    row_input = lax.dot_general(d_joined, gate_matrix, last, preferred_element_type=F32).astype(BF)
    back = jnp.concatenate(
        [expert_out.reshape(plane, count, width), row_input.reshape(plane, count, width)], axis=1
    )
    back = lax.all_to_all(back, PLANE, 0, 0, tiled=True)
    back_out = back[:, :count].reshape(plane, micro, nz, 2, width)
    back_grad = back[:, count:].reshape(plane, micro, nz, 2, width)
    scaled = pick * weight[..., None]
    scaled_high = scaled.astype(BF)
    scaled_low = (scaled - scaled_high.astype(F32)).astype(BF)
    form = "smtdr,dmsrw->smtw"
    part_out = jnp.einsum(form, scaled_high, back_out, preferred_element_type=F32) + jnp.einsum(
        form, scaled_low, back_out, preferred_element_type=F32
    )
    part_grad = jnp.einsum(form, pick_b, back_grad, preferred_element_type=F32)
    part = jnp.stack([part_out, part_grad], axis=1)
    total = part[0]
    for s in range(1, nz):
        total = total + along_z(part[s].astype(BF), -s).astype(F32)
    total = total.astype(BF)
    return (total[0], total[1], resident_gate, resident_down)


def solution(mesh):
    devices = mesh.devices.reshape(4, 4, 4, 4, 2)
    fine = Mesh(devices, ("dp", "y", "x", "z", "c"))
    tokens = P(None, ("dp",) + EXPERT, None)
    placed = (
        tokens,
        tokens,
        tokens,
        tokens,
        P(),
        P(EXPERT, "dp", None, None),
        P(EXPERT, "dp", None),
    )
    return jax.shard_map(
        local,
        mesh=fine,
        in_specs=placed,
        out_specs=(tokens, tokens, P(EXPERT, "dp", None, None), P(EXPERT, "dp", None)),
        check_vma=False,
    )
```

profile of v0, /device:TPU:117, one launch (start us, length us, event | category | flops | bytes accessed | tf_op | source)
XLA Modules:
  0.0 333.7 jit_solution(6145874898485073797)
XLA Ops:
  8.6 8.8 %collective-permute-start = (f32[2,16,16]{1,2,0:T(8,128)S(1)}, f32[2,16,16]{1,2,0:T(8,128)S(1)}, u32[]{:S(2)}, u32[]{:S(2)}) collective-permute-start(f32[2,16,16]{1,2,0:T(8,128)S(1)} %get-tuple-element.18), channel_id=1, source_target_pairs={{0,2},{2,4},{4,6},{6,0},{1,3},{3,5},{5,7},{7,1},{8,10},{10,12},{12... | collective-permute-start | bytes 6152 | tf_op jit(solution)/shard_map/ppermute | solution.py:14
  17.4 7.9 %collective-permute-start.1 = (f32[2,16,16]{1,2,0:T(8,128)S(1)}, f32[2,16,16]{1,2,0:T(8,128)S(1)}, u32[]{:S(2)}, u32[]{:S(2)}) collective-permute-start(f32[2,16,16]{1,2,0:T(8,128)S(1)} %get-tuple-element.18), channel_id=1, source_target_pairs={{0,4},{2,6},{4,0},{6,2},{1,5},{3,7},{5,1},{7,3},{8,12},{10,14},{12... | collective-permute-start | bytes 6152 | tf_op jit(solution)/shard_map/ppermute | solution.py:14
  25.4 5.2 %collective-permute-start.2 = (f32[2,16,16]{1,2,0:T(8,128)S(1)}, f32[2,16,16]{1,2,0:T(8,128)S(1)}, u32[]{:S(2)}, u32[]{:S(2)}) collective-permute-start(f32[2,16,16]{1,2,0:T(8,128)S(1)} %get-tuple-element.18), channel_id=1, source_target_pairs={{0,6},{2,0},{4,2},{6,4},{1,7},{3,1},{5,3},{7,5},{8,14},{10,8},{12,... | collective-permute-start | bytes 6152 | tf_op jit(solution)/shard_map/ppermute | solution.py:14
  34.1 4.0 %collective-permute-start.3 = (bf16[2,2,16,2048]{3,2,1,0:T(8,128)(2,1)S(1)}, bf16[2,2,16,2048]{3,2,1,0:T(8,128)(2,1)S(1)}, u32[]{:S(2)}, u32[]{:S(2)}) collective-permute-start(bf16[2,2,16,2048]{3,2,1,0:T(8,128)(2,1)S(1)} %get-tuple-element.16), channel_id=1, source_target_pairs={{0,2},{2,4},{4,6},{6,0},{1,3},{3,5},{5,7},{7,1},{8,10},{10,12},{12... | collective-permute-start | bytes 786440 | tf_op jit(solution)/shard_map/ppermute | solution.py:14
  38.1 6.1 %collective-permute-start.4 = (bf16[2,2,16,2048]{3,2,1,0:T(8,128)(2,1)S(1)}, bf16[2,2,16,2048]{3,2,1,0:T(8,128)(2,1)S(1)}, u32[]{:S(2)}, u32[]{:S(2)}) collective-permute-start(bf16[2,2,16,2048]{3,2,1,0:T(8,128)(2,1)S(1)} %get-tuple-element.16), channel_id=1, source_target_pairs={{0,4},{2,6},{4,0},{6,2},{1,5},{3,7},{5,1},{7,3},{8,12},{10,14},{12... | collective-permute-start | bytes 786440 | tf_op jit(solution)/shard_map/ppermute | solution.py:14
  44.2 2.9 collective-permute-start.5
  48.3 14.5 %collective-permute-done.3 = bf16[2,2,16,2048]{3,2,1,0:T(8,128)(2,1)S(1)} collective-permute-done((bf16[2,2,16,2048]{3,2,1,0:T(8,128)(2,1)S(1)}, bf16[2,2,16,2048]{3,2,1,0:T(8,128)(2,1)S(1)}, u32[]{:S(2)}, u32[]{:S(2)}) %collective-permute-start.3) | collective-permute-done | bytes 262176 | tf_op jit(solution)/shard_map/ppermute | solution.py:14
  62.8 11.7 %collective-permute-done.4 = bf16[2,2,16,2048]{3,2,1,0:T(8,128)(2,1)S(1)} collective-permute-done((bf16[2,2,16,2048]{3,2,1,0:T(8,128)(2,1)S(1)}, bf16[2,2,16,2048]{3,2,1,0:T(8,128)(2,1)S(1)}, u32[]{:S(2)}, u32[]{:S(2)}) %collective-permute-start.4) | collective-permute-done | bytes 262176 | tf_op jit(solution)/shard_map/ppermute | solution.py:14
  74.5 16.0 %collective-permute-done.5 = bf16[2,2,16,2048]{3,2,1,0:T(8,128)(2,1)S(1)} collective-permute-done((bf16[2,2,16,2048]{3,2,1,0:T(8,128)(2,1)S(1)}, bf16[2,2,16,2048]{3,2,1,0:T(8,128)(2,1)S(1)}, u32[]{:S(2)}, u32[]{:S(2)}) %collective-permute-start.5) | collective-permute-done | bytes 262176 | tf_op jit(solution)/shard_map/ppermute | solution.py:14
  95.2 59.0 %all_to_all.10 = bf16[32,32,2048]{2,1,0:T(8,128)(2,1)S(1)} all-to-all(bf16[32,32,2048]{2,1,0:T(8,128)(2,1)S(1)} %pad_maximum_fusion), channel_id=1, replica_groups=mesh['dp'=4,'y'=4,'x'=4,'z'=4,'c'=2] {'y','x','c'}, dimensions={0} | all-to-all | bytes 8388608 | tf_op jit(solution)/shard_map/all_to_all | solution.py:66
  155.9 10.1 %all-gather.2.cloned.1.call-done = bf16[2048,1152]{1,0:T(8,128)(2,1)} async-done(((bf16[512,1152]{1,0:T(8,128)(2,1)}), bf16[2048,1152]{1,0:T(8,128)(2,1)}) %all-gather.2.cloned.1.call-update) | async-done | bytes 4718608 | tf_op jit(solution)/shard_map/all_gather | solution.py:39
  166.0 4.5 %fusion.2 = f32[512,768]{1,0:T(8,128)S(1)} fusion(bf16[512,2048]{1,0:T(8,128)(2,1)} %bitcast.117, bf16[2048,1152]{1,0:T(8,128)(2,1)} %all-gather.2.cloned.1.call-done), kind=kOutput, calls=%fused_computation.8 | convolution fusion | flops 1610612736 | bytes 6815744 | tf_op jit(solution)/shard_map/dot_general | solution.py:69
  175.1 2.6 pad_maximum_fusion.1
  177.7 7.8 %all-to-all-start.1 = ((bf16[32,32,2048]{2,1,0:T(8,128)(2,1)}), bf16[32,32,2048]{2,1,0:T(8,128)(2,1)}, u32[]{:S(2)}, u32[]{:S(2)}) async-start(bf16[32,32,2048]{2,1,0:T(8,128)(2,1)} %pad_maximum_fusion.1), calls=%async_computation.1 | async-start | bytes 8388608 | tf_op jit(solution)/shard_map/all_to_all | solution.py:84
  185.5 2.2 collective-permute-start.10
  187.7 4.6 %collective-permute-start.9 = (bf16[1,512,2,384]{3,2,1,0:T(2,128)(2,1)S(1)}, bf16[1,512,2,384]{3,2,1,0:T(2,128)(2,1)S(1)}, u32[]{:S(2)}, u32[]{:S(2)}) collective-permute-start(bf16[1,512,2,384]{3,2,1,0:T(2,128)(2,1)S(1)} %copy-done), channel_id=1, source_target_pairs={{0,64},{32,96},{64,0},{96,32},{1,65},{33,97},{65,1},{97,33},{2,66}... | collective-permute-start | bytes 2359304 | tf_op jit(solution)/shard_map/ppermute | solution.py:30
  193.6 46.3 %collective-permute-done.10 = bf16[1,512,384]{2,1,0:T(8,128)(2,1)S(1)} collective-permute-done((bf16[1,512,384]{2,1,0:T(8,128)(2,1)S(1)}, bf16[1,512,384]{2,1,0:T(8,128)(2,1)S(1)}, u32[]{:S(2)}, u32[]{:S(2)}) %collective-permute-start.10) | collective-permute-done | bytes 393248 | tf_op jit(solution)/shard_map/ppermute | solution.py:31
  240.7 16.6 %all-to-all-done.1 = bf16[32,32,2048]{2,1,0:T(8,128)(2,1)} async-done(((bf16[32,32,2048]{2,1,0:T(8,128)(2,1)}), bf16[32,32,2048]{2,1,0:T(8,128)(2,1)}, u32[]{:S(2)}, u32[]{:S(2)}) %all-to-all-start.1) | async-done | bytes 4194336 | tf_op jit(solution)/shard_map/all_to_all | solution.py:84
  257.3 2.7 fusion.62
  264.2 2.7 collective-permute-start.6
  266.9 10.3 %collective-permute-start.7 = (bf16[2,2,16,2048]{3,2,1,0:T(8,128)(2,1)S(1)}, bf16[2,2,16,2048]{3,2,1,0:T(8,128)(2,1)S(1)}, u32[]{:S(2)}, u32[]{:S(2)}) collective-permute-start(bf16[2,2,16,2048]{3,2,1,0:T(8,128)(2,1)S(1)} %get-tuple-element.12), channel_id=1, source_target_pairs={{0,4},{2,6},{4,0},{6,2},{1,5},{3,7},{5,1},{7,3},{8,12},{10,14},{12... | collective-permute-start | bytes 786440 | tf_op jit(solution)/shard_map/ppermute | solution.py:14
  277.2 2.9 collective-permute-start.8
  281.1 39.5 %collective-permute-done.7 = bf16[2,2,16,2048]{3,2,1,0:T(8,128)(2,1)S(1)} collective-permute-done((bf16[2,2,16,2048]{3,2,1,0:T(8,128)(2,1)S(1)}, bf16[2,2,16,2048]{3,2,1,0:T(8,128)(2,1)S(1)}, u32[]{:S(2)}, u32[]{:S(2)}) %collective-permute-start.7) | collective-permute-done | bytes 262176 | tf_op jit(solution)/shard_map/ppermute | solution.py:14
  320.6 5.4 %collective-permute-done.8 = bf16[2,2,16,2048]{3,2,1,0:T(8,128)(2,1)S(1)} collective-permute-done((bf16[2,2,16,2048]{3,2,1,0:T(8,128)(2,1)S(1)}, bf16[2,2,16,2048]{3,2,1,0:T(8,128)(2,1)S(1)}, u32[]{:S(2)}, u32[]{:S(2)}) %collective-permute-start.8) | collective-permute-done | bytes 262176 | tf_op jit(solution)/shard_map/ppermute | solution.py:14
  (57 shorter events, 24.5 us)
Async XLA Ops:
  7.2 158.9 %all-gather.2.cloned.1.call-start = ((), (), s32[]{:S(2)}) async-start(), calls=%async_computation.2 | async-start | bytes 5898240 | tf_op jit(solution)/shard_map/all_gather | solution.py:39
  8.6 35.6 %collective-permute-start = (f32[2,16,16]{1,2,0:T(8,128)S(1)}, f32[2,16,16]{1,2,0:T(8,128)S(1)}, u32[]{:S(2)}, u32[]{:S(2)}) collective-permute-start(f32[2,16,16]{1,2,0:T(8,128)S(1)} %get-tuple-element.18), channel_id=1, source_target_pairs={{0,2},{2,4},{4,6},{6,0},{1,3},{3,5},{5,7},{7,1},{8,10},{10,12},{12... | collective-permute-start | bytes 6152 | tf_op jit(solution)/shard_map/ppermute | solution.py:14
  17.4 29.7 %collective-permute-start.1 = (f32[2,16,16]{1,2,0:T(8,128)S(1)}, f32[2,16,16]{1,2,0:T(8,128)S(1)}, u32[]{:S(2)}, u32[]{:S(2)}) collective-permute-start(f32[2,16,16]{1,2,0:T(8,128)S(1)} %get-tuple-element.18), channel_id=1, source_target_pairs={{0,4},{2,6},{4,0},{6,2},{1,5},{3,7},{5,1},{7,3},{8,12},{10,14},{12... | collective-permute-start | bytes 6152 | tf_op jit(solution)/shard_map/ppermute | solution.py:14
  25.4 21.7 %collective-permute-start.2 = (f32[2,16,16]{1,2,0:T(8,128)S(1)}, f32[2,16,16]{1,2,0:T(8,128)S(1)}, u32[]{:S(2)}, u32[]{:S(2)}) collective-permute-start(f32[2,16,16]{1,2,0:T(8,128)S(1)} %get-tuple-element.18), channel_id=1, source_target_pairs={{0,6},{2,0},{4,2},{6,4},{1,7},{3,1},{5,3},{7,5},{8,14},{10,8},{12,... | collective-permute-start | bytes 6152 | tf_op jit(solution)/shard_map/ppermute | solution.py:14
  31.8 2.2 copy-start.2
  31.8 2.2 copy-start.3
  34.1 28.8 %collective-permute-start.3 = (bf16[2,2,16,2048]{3,2,1,0:T(8,128)(2,1)S(1)}, bf16[2,2,16,2048]{3,2,1,0:T(8,128)(2,1)S(1)}, u32[]{:S(2)}, u32[]{:S(2)}) collective-permute-start(bf16[2,2,16,2048]{3,2,1,0:T(8,128)(2,1)S(1)} %get-tuple-element.16), channel_id=1, source_target_pairs={{0,2},{2,4},{4,6},{6,0},{1,3},{3,5},{5,7},{7,1},{8,10},{10,12},{12... | collective-permute-start | bytes 786440 | tf_op jit(solution)/shard_map/ppermute | solution.py:14
  38.1 36.4 %collective-permute-start.4 = (bf16[2,2,16,2048]{3,2,1,0:T(8,128)(2,1)S(1)}, bf16[2,2,16,2048]{3,2,1,0:T(8,128)(2,1)S(1)}, u32[]{:S(2)}, u32[]{:S(2)}) collective-permute-start(bf16[2,2,16,2048]{3,2,1,0:T(8,128)(2,1)S(1)} %get-tuple-element.16), channel_id=1, source_target_pairs={{0,4},{2,6},{4,0},{6,2},{1,5},{3,7},{5,1},{7,3},{8,12},{10,14},{12... | collective-permute-start | bytes 786440 | tf_op jit(solution)/shard_map/ppermute | solution.py:14
  44.2 46.3 %collective-permute-start.5 = (bf16[2,2,16,2048]{3,2,1,0:T(8,128)(2,1)S(1)}, bf16[2,2,16,2048]{3,2,1,0:T(8,128)(2,1)S(1)}, u32[]{:S(2)}, u32[]{:S(2)}) collective-permute-start(bf16[2,2,16,2048]{3,2,1,0:T(8,128)(2,1)S(1)} %get-tuple-element.16), channel_id=1, source_target_pairs={{0,6},{2,0},{4,2},{6,4},{1,7},{3,1},{5,3},{7,5},{8,14},{10,8},{12,... | collective-permute-start | bytes 786440 | tf_op jit(solution)/shard_map/ppermute | solution.py:14
  166.0 4.5 %copy-start.4 = (bf16[2048,1152]{1,0:T(8,128)(2,1)S(1)}, bf16[2048,1152]{1,0:T(8,128)(2,1)}, u32[]{:S(2)}) copy-start(bf16[2048,1152]{1,0:T(8,128)(2,1)} %all-gather.2.cloned.1.call-done) | copy-start | bytes 14155780
  177.7 7.8 %copy-start.1 = (bf16[1,512,384]{2,1,0:T(8,128)(2,1)S(1)}, bf16[1,512,384]{2,1,0:T(8,128)(2,1)}, u32[]{:S(2)}) copy-start(bf16[1,512,384]{2,1,0:T(8,128)(2,1)} %param.13) | copy-start | bytes 1179652
  177.7 10.0 %copy-start = (bf16[1,512,2,384]{3,2,1,0:T(2,128)(2,1)S(1)}, bf16[1,512,2,384]{3,2,1,0:T(2,128)(2,1)}, u32[]{:S(2)}) copy-start(bf16[1,512,2,384]{3,2,1,0:T(2,128)(2,1)} %param.12) | copy-start | bytes 2359300
  177.7 14.7 %copy-start.5 = (s32[64]{0:T(128)S(1)}, s32[64]{0:T(128)}, u32[]{:S(2)}) copy-start(s32[64]{0:T(128)} %param.11) | copy-start | bytes 772
  177.7 79.6 %all-to-all-start.1 = ((bf16[32,32,2048]{2,1,0:T(8,128)(2,1)}), bf16[32,32,2048]{2,1,0:T(8,128)(2,1)}, u32[]{:S(2)}, u32[]{:S(2)}) async-start(bf16[32,32,2048]{2,1,0:T(8,128)(2,1)} %pad_maximum_fusion.1), calls=%async_computation.1 | async-start | bytes 8388608 | tf_op jit(solution)/shard_map/all_to_all | solution.py:84
  185.5 54.4 %collective-permute-start.10 = (bf16[1,512,384]{2,1,0:T(8,128)(2,1)S(1)}, bf16[1,512,384]{2,1,0:T(8,128)(2,1)S(1)}, u32[]{:S(2)}, u32[]{:S(2)}) collective-permute-start(bf16[1,512,384]{2,1,0:T(8,128)(2,1)S(1)} %copy-done.1), channel_id=1, source_target_pairs={{0,64},{32,96},{64,0},{96,32},{1,65},{33,97},{65,1},{97,33},{2,66}... | collective-permute-start | bytes 1179656 | tf_op jit(solution)/shard_map/ppermute | solution.py:31
  187.7 92.5 %collective-permute-start.9 = (bf16[1,512,2,384]{3,2,1,0:T(2,128)(2,1)S(1)}, bf16[1,512,2,384]{3,2,1,0:T(2,128)(2,1)S(1)}, u32[]{:S(2)}, u32[]{:S(2)}) collective-permute-start(bf16[1,512,2,384]{3,2,1,0:T(2,128)(2,1)S(1)} %copy-done), channel_id=1, source_target_pairs={{0,64},{32,96},{64,0},{96,32},{1,65},{33,97},{65,1},{97,33},{2,66}... | collective-permute-start | bytes 2359304 | tf_op jit(solution)/shard_map/ppermute | solution.py:30
  264.2 16.9 %collective-permute-start.6 = (bf16[2,2,16,2048]{3,2,1,0:T(8,128)(2,1)S(1)}, bf16[2,2,16,2048]{3,2,1,0:T(8,128)(2,1)S(1)}, u32[]{:S(2)}, u32[]{:S(2)}) collective-permute-start(bf16[2,2,16,2048]{3,2,1,0:T(8,128)(2,1)S(1)} %get-tuple-element.10), channel_id=1, source_target_pairs={{0,6},{2,0},{4,2},{6,4},{1,7},{3,1},{5,3},{7,5},{8,14},{10,8},{12,... | collective-permute-start | bytes 786440 | tf_op jit(solution)/shard_map/ppermute | solution.py:14
  266.9 53.8 %collective-permute-start.7 = (bf16[2,2,16,2048]{3,2,1,0:T(8,128)(2,1)S(1)}, bf16[2,2,16,2048]{3,2,1,0:T(8,128)(2,1)S(1)}, u32[]{:S(2)}, u32[]{:S(2)}) collective-permute-start(bf16[2,2,16,2048]{3,2,1,0:T(8,128)(2,1)S(1)} %get-tuple-element.12), channel_id=1, source_target_pairs={{0,4},{2,6},{4,0},{6,2},{1,5},{3,7},{5,1},{7,3},{8,12},{10,14},{12... | collective-permute-start | bytes 786440 | tf_op jit(solution)/shard_map/ppermute | solution.py:14
  277.2 48.8 %collective-permute-start.8 = (bf16[2,2,16,2048]{3,2,1,0:T(8,128)(2,1)S(1)}, bf16[2,2,16,2048]{3,2,1,0:T(8,128)(2,1)S(1)}, u32[]{:S(2)}, u32[]{:S(2)}) collective-permute-start(bf16[2,2,16,2048]{3,2,1,0:T(8,128)(2,1)S(1)} %get-tuple-element.11), channel_id=1, source_target_pairs={{0,2},{2,4},{4,6},{6,0},{1,3},{3,5},{5,7},{7,1},{8,10},{10,12},{12... | collective-permute-start | bytes 786440 | tf_op jit(solution)/shard_map/ppermute | solution.py:14
Sparse Core Ops, SparseCore 0:
  34.1 131.8 all-gather.1
where the time goes:
time: 334 us
  waiting for transfers between devices  160 us (48%)
  starting transfers between devices  65.4 us (20%)
  blocking collectives  59 us (18%)
  between operations  15.1 us (5%)
  matrix products  12.4 us (4%)
  local copies, waits for them, and re-layouts  11.4 us (3%)
  other arithmetic  10.4 us (3%)
    ppermute x9, waiting for transfers between devices, along_z(): lax.ppermute(value, 'z', [(i, (i + shift) % count) for i in range(count)])  87.1 us
    all_to_all x1, blocking collectives, local(): rows = lax.all_to_all(rows, PLANE, 0, 0, tiled=True)  59 us
    ppermute x9, starting transfers between devices, along_z(): lax.ppermute(value, 'z', [(i, (i + shift) % count) for i in range(count)])  50.8 us
    ppermute x1, waiting for transfers between devices, local(): other_down = lax.ppermute(down_t, 'y', pairs)  46.3 us
    all_to_all x1, waiting for transfers between devices, local(): back = lax.all_to_all(back, PLANE, 0, 0, tiled=True)  16.6 us
    all_gather x1, waiting for transfers between devices, local(): weights = lax.all_gather(weights, 'dp', axis=0, tiled=True)  10.1 us
    all_to_all x1, starting transfers between devices, local(): back = lax.all_to_all(back, PLANE, 0, 0, tiled=True)  7.81 us
  transfers between devices with their start and end apart: 13, of which 8 were waited for; matrix products, arithmetic and copies ran while one was open for 6% of the time, Pallas kernels for 0%

commit v1 on v0

--- a/solution.py
+++ b/solution.py
@@ -36,7 +36,9 @@
     facts = jnp.stack([facts] + [along_z(facts, s) for s in range(1, nz)])
     column = jnp.stack([mine] + [along_z(mine, s) for s in range(1, nz)])
     weights = jnp.concatenate([gate_up.reshape(-1, 2 * hid), down_t.reshape(-1, hid)], axis=1)
-    weights = lax.all_gather(weights, "dp", axis=0, tiled=True)
+    weights = jnp.concatenate(
+        lax.all_to_all(jnp.stack([weights] * lax.axis_size("dp")), "dp", 0, 0), axis=0
+    )
     gate_matrix = weights[:, : 2 * hid]
     down_matrix = weights[:, 2 * hid :]
     ids = facts[..., :top].astype(jnp.int32)

time: 334 us -> 424 us (1.27)
  the two profiles are of different devices: /device:TPU:117 before, /device:TPU:85 now
where the time goes in v1:
time: 424 us; the launch traced here: 423 us
  waiting for transfers between devices  288 us (68%)
  starting transfers between devices  90.6 us (21%)
  matrix products  16.5 us (4%)
  local copies, waits for them, and re-layouts  14.9 us (4%)
  other arithmetic  11.3 us (3%)
    all_to_all x1, waiting for transfers between devices, local(): lax.all_to_all(jnp.stack([weights] * lax.axis_size('dp')), 'dp', 0, 0)  97.3 us
    ppermute x9, waiting for transfers between devices, along_z(): lax.ppermute(value, 'z', [(i, (i + shift) % count) for i in range(count)])  80.9 us
    ppermute x9, starting transfers between devices, along_z(): lax.ppermute(value, 'z', [(i, (i + shift) % count) for i in range(count)])  51.4 us
    all_to_all x1, waiting for transfers between devices, local(): rows = lax.all_to_all(rows, PLANE, 0, 0, tiled=True)  46.8 us
    ppermute x1, waiting for transfers between devices, local(): other_down = lax.ppermute(down_t, 'y', pairs)  46.3 us
    all_to_all x1, starting transfers between devices, local(): rows = lax.all_to_all(rows, PLANE, 0, 0, tiled=True)  17.9 us
    all_to_all x1, waiting for transfers between devices, local(): back = lax.all_to_all(back, PLANE, 0, 0, tiled=True)  16.6 us
    all_to_all x1, starting transfers between devices, local(): back = lax.all_to_all(back, PLANE, 0, 0, tiled=True)  9.35 us
  transfers between devices with their start and end apart: 14, of which 9 were waited for; matrix products, arithmetic and copies ran while one was open for 4% of the time, Pallas kernels for 0%

profile of v1, /device:TPU:85, one launch (start us, length us, event | category | flops | bytes accessed | tf_op | source)
XLA Modules:
  0.0 422.8 jit_solution(8788565458360035182)
XLA Ops:
  1.6 10.7 %collective-permute-start.5 = (bf16[2,2,16,2048]{3,2,1,0:T(8,128)(2,1)S(1)}, bf16[2,2,16,2048]{3,2,1,0:T(8,128)(2,1)S(1)}, u32[]{:S(2)}, u32[]{:S(2)}) collective-permute-start(bf16[2,2,16,2048]{3,2,1,0:T(8,128)(2,1)S(1)} %get-tuple-element.16), channel_id=1, source_target_pairs={{0,6},{2,0},{4,2},{6,4},{1,7},{3,1},{5,3},{7,5},{8,14},{10,8},{12,... | collective-permute-start | bytes 786440 | tf_op jit(solution)/shard_map/ppermute | solution.py:14
  12.3 5.2 %collective-permute-start.4 = (bf16[2,2,16,2048]{3,2,1,0:T(8,128)(2,1)S(1)}, bf16[2,2,16,2048]{3,2,1,0:T(8,128)(2,1)S(1)}, u32[]{:S(2)}, u32[]{:S(2)}) collective-permute-start(bf16[2,2,16,2048]{3,2,1,0:T(8,128)(2,1)S(1)} %get-tuple-element.16), channel_id=1, source_target_pairs={{0,4},{2,6},{4,0},{6,2},{1,5},{3,7},{5,1},{7,3},{8,12},{10,14},{12... | collective-permute-start | bytes 786440 | tf_op jit(solution)/shard_map/ppermute | solution.py:14
  20.8 12.1 %collective-permute-start.1 = (f32[2,16,16]{1,2,0:T(8,128)S(1)}, f32[2,16,16]{1,2,0:T(8,128)S(1)}, u32[]{:S(2)}, u32[]{:S(2)}) collective-permute-start(f32[2,16,16]{1,2,0:T(8,128)S(1)} %get-tuple-element.18), channel_id=1, source_target_pairs={{0,4},{2,6},{4,0},{6,2},{1,5},{3,7},{5,1},{7,3},{8,12},{10,14},{12... | collective-permute-start | bytes 6152 | tf_op jit(solution)/shard_map/ppermute | solution.py:14
  32.9 4.0 collective-permute-start
  36.9 17.7 %collective-permute-done.2 = f32[2,16,16]{1,2,0:T(8,128)S(1)} collective-permute-done((f32[2,16,16]{1,2,0:T(8,128)S(1)}, f32[2,16,16]{1,2,0:T(8,128)S(1)}, u32[]{:S(2)}, u32[]{:S(2)}) %collective-permute-start.2) | collective-permute-done | bytes 2080 | tf_op jit(solution)/shard_map/ppermute | solution.py:14
  57.8 18.5 %collective-permute-done.3 = bf16[2,2,16,2048]{3,2,1,0:T(8,128)(2,1)S(1)} collective-permute-done((bf16[2,2,16,2048]{3,2,1,0:T(8,128)(2,1)S(1)}, bf16[2,2,16,2048]{3,2,1,0:T(8,128)(2,1)S(1)}, u32[]{:S(2)}, u32[]{:S(2)}) %collective-permute-start.3) | collective-permute-done | bytes 262176 | tf_op jit(solution)/shard_map/ppermute | solution.py:14
  83.0 17.9 %all-to-all-start = ((bf16[32,32,2048]{2,1,0:T(8,128)(2,1)}), bf16[32,32,2048]{2,1,0:T(8,128)(2,1)}, u32[]{:S(2)}, u32[]{:S(2)}) async-start(bf16[32,32,2048]{2,1,0:T(8,128)(2,1)} %pad_maximum_fusion), calls=%async_computation | async-start | bytes 8388608 | tf_op jit(solution)/shard_map/all_to_all | solution.py:68
  101.1 46.8 %all-to-all-done = bf16[32,32,2048]{2,1,0:T(8,128)(2,1)} async-done(((bf16[32,32,2048]{2,1,0:T(8,128)(2,1)}), bf16[32,32,2048]{2,1,0:T(8,128)(2,1)}, u32[]{:S(2)}, u32[]{:S(2)}) %all-to-all-start) | async-done | bytes 4194336 | tf_op jit(solution)/shard_map/all_to_all | solution.py:68
  150.4 5.1 %all-to-all-start.1 = ((bf16[4,512,1152]{2,1,0:T(8,128)(2,1)}), bf16[4,512,1152]{2,1,0:T(8,128)(2,1)}, u32[]{:S(2)}, u32[]{:S(2)}) async-start(bf16[4,512,1152]{2,1,0:T(8,128)(2,1)} %stack.68), calls=%async_computation.1 | async-start | bytes 9437184 | tf_op jit(solution)/shard_map/all_to_all | solution.py:40
  155.5 4.0 fusion.63
  159.5 97.3 %all-to-all-done.1 = bf16[4,512,1152]{2,1,0:T(8,128)(2,1)} async-done(((bf16[4,512,1152]{2,1,0:T(8,128)(2,1)}), bf16[4,512,1152]{2,1,0:T(8,128)(2,1)}, u32[]{:S(2)}, u32[]{:S(2)}) %all-to-all-start.1) | async-done | bytes 4718624 | tf_op jit(solution)/shard_map/all_to_all | solution.py:40
  256.8 3.7 fusion.2
  260.5 2.9 convolution_convert_fusion.1
  263.4 2.9 multiply_convert_fusion.1
  266.2 3.7 convolution_convert_fusion
  272.5 9.3 %all-to-all-start.2 = ((bf16[32,32,2048]{2,1,0:T(8,128)(2,1)}), bf16[32,32,2048]{2,1,0:T(8,128)(2,1)}, u32[]{:S(2)}, u32[]{:S(2)}) async-start(bf16[32,32,2048]{2,1,0:T(8,128)(2,1)} %pad_maximum_fusion.1), calls=%async_computation.2 | async-start | bytes 8388608 | tf_op jit(solution)/shard_map/all_to_all | solution.py:86
  284.1 4.6 %collective-permute-start.9 = (bf16[1,512,2,384]{3,2,1,0:T(2,128)(2,1)S(1)}, bf16[1,512,2,384]{3,2,1,0:T(2,128)(2,1)S(1)}, u32[]{:S(2)}, u32[]{:S(2)}) collective-permute-start(bf16[1,512,2,384]{3,2,1,0:T(2,128)(2,1)S(1)} %copy-done), channel_id=1, source_target_pairs={{0,64},{32,96},{64,0},{96,32},{1,65},{33,97},{65,1},{97,33},{2,66}... | collective-permute-start | bytes 2359304 | tf_op jit(solution)/shard_map/ppermute | solution.py:30
  290.0 46.3 %collective-permute-done.10 = bf16[1,512,384]{2,1,0:T(8,128)(2,1)S(1)} collective-permute-done((bf16[1,512,384]{2,1,0:T(8,128)(2,1)S(1)}, bf16[1,512,384]{2,1,0:T(8,128)(2,1)S(1)}, u32[]{:S(2)}, u32[]{:S(2)}) %collective-permute-start.10) | collective-permute-done | bytes 393248 | tf_op jit(solution)/shard_map/ppermute | solution.py:31
  337.1 16.6 %all-to-all-done.2 = bf16[32,32,2048]{2,1,0:T(8,128)(2,1)} async-done(((bf16[32,32,2048]{2,1,0:T(8,128)(2,1)}), bf16[32,32,2048]{2,1,0:T(8,128)(2,1)}, u32[]{:S(2)}, u32[]{:S(2)}) %all-to-all-start.2) | async-done | bytes 4194336 | tf_op jit(solution)/shard_map/all_to_all | solution.py:86
  362.5 9.4 %collective-permute-start.7 = (bf16[2,2,16,2048]{3,2,1,0:T(8,128)(2,1)S(1)}, bf16[2,2,16,2048]{3,2,1,0:T(8,128)(2,1)S(1)}, u32[]{:S(2)}, u32[]{:S(2)}) collective-permute-start(bf16[2,2,16,2048]{3,2,1,0:T(8,128)(2,1)S(1)} %get-tuple-element.12), channel_id=1, source_target_pairs={{0,4},{2,6},{4,0},{6,2},{1,5},{3,7},{5,1},{7,3},{8,12},{10,14},{12... | collective-permute-start | bytes 786440 | tf_op jit(solution)/shard_map/ppermute | solution.py:14
  372.0 4.3 %collective-permute-start.6 = (bf16[2,2,16,2048]{3,2,1,0:T(8,128)(2,1)S(1)}, bf16[2,2,16,2048]{3,2,1,0:T(8,128)(2,1)S(1)}, u32[]{:S(2)}, u32[]{:S(2)}) collective-permute-start(bf16[2,2,16,2048]{3,2,1,0:T(8,128)(2,1)S(1)} %get-tuple-element.10), channel_id=1, source_target_pairs={{0,6},{2,0},{4,2},{6,4},{1,7},{3,1},{5,3},{7,5},{8,14},{10,8},{12,... | collective-permute-start | bytes 786440 | tf_op jit(solution)/shard_map/ppermute | solution.py:14
  377.3 5.3 %collective-permute-done.8 = bf16[2,2,16,2048]{3,2,1,0:T(8,128)(2,1)S(1)} collective-permute-done((bf16[2,2,16,2048]{3,2,1,0:T(8,128)(2,1)S(1)}, bf16[2,2,16,2048]{3,2,1,0:T(8,128)(2,1)S(1)}, u32[]{:S(2)}, u32[]{:S(2)}) %collective-permute-start.8) | collective-permute-done | bytes 262176 | tf_op jit(solution)/shard_map/ppermute | solution.py:14
  382.6 10.0 %collective-permute-done.7 = bf16[2,2,16,2048]{3,2,1,0:T(8,128)(2,1)S(1)} collective-permute-done((bf16[2,2,16,2048]{3,2,1,0:T(8,128)(2,1)S(1)}, bf16[2,2,16,2048]{3,2,1,0:T(8,128)(2,1)S(1)}, u32[]{:S(2)}, u32[]{:S(2)}) %collective-permute-start.7) | collective-permute-done | bytes 262176 | tf_op jit(solution)/shard_map/ppermute | solution.py:14
  392.7 29.3 %collective-permute-done.6 = bf16[2,2,16,2048]{3,2,1,0:T(8,128)(2,1)S(1)} collective-permute-done((bf16[2,2,16,2048]{3,2,1,0:T(8,128)(2,1)S(1)}, bf16[2,2,16,2048]{3,2,1,0:T(8,128)(2,1)S(1)}, u32[]{:S(2)}, u32[]{:S(2)}) %collective-permute-start.6) | collective-permute-done | bytes 262176 | tf_op jit(solution)/shard_map/ppermute | solution.py:14
  (54 shorter events, 33.6 us)
Async XLA Ops:
  1.6 56.1 %collective-permute-start.5 = (bf16[2,2,16,2048]{3,2,1,0:T(8,128)(2,1)S(1)}, bf16[2,2,16,2048]{3,2,1,0:T(8,128)(2,1)S(1)}, u32[]{:S(2)}, u32[]{:S(2)}) collective-permute-start(bf16[2,2,16,2048]{3,2,1,0:T(8,128)(2,1)S(1)} %get-tuple-element.16), channel_id=1, source_target_pairs={{0,6},{2,0},{4,2},{6,4},{1,7},{3,1},{5,3},{7,5},{8,14},{10,8},{12,... | collective-permute-start | bytes 786440 | tf_op jit(solution)/shard_map/ppermute | solution.py:14
  12.3 45.5 %collective-permute-start.4 = (bf16[2,2,16,2048]{3,2,1,0:T(8,128)(2,1)S(1)}, bf16[2,2,16,2048]{3,2,1,0:T(8,128)(2,1)S(1)}, u32[]{:S(2)}, u32[]{:S(2)}) collective-permute-start(bf16[2,2,16,2048]{3,2,1,0:T(8,128)(2,1)S(1)} %get-tuple-element.16), channel_id=1, source_target_pairs={{0,4},{2,6},{4,0},{6,2},{1,5},{3,7},{5,1},{7,3},{8,12},{10,14},{12... | collective-permute-start | bytes 786440 | tf_op jit(solution)/shard_map/ppermute | solution.py:14
  18.9 35.8 %collective-permute-start.2 = (f32[2,16,16]{1,2,0:T(8,128)S(1)}, f32[2,16,16]{1,2,0:T(8,128)S(1)}, u32[]{:S(2)}, u32[]{:S(2)}) collective-permute-start(f32[2,16,16]{1,2,0:T(8,128)S(1)} %get-tuple-element.18), channel_id=1, source_target_pairs={{0,6},{2,0},{4,2},{6,4},{1,7},{3,1},{5,3},{7,5},{8,14},{10,8},{12,... | collective-permute-start | bytes 6152 | tf_op jit(solution)/shard_map/ppermute | solution.py:14
  20.8 35.8 %collective-permute-start.1 = (f32[2,16,16]{1,2,0:T(8,128)S(1)}, f32[2,16,16]{1,2,0:T(8,128)S(1)}, u32[]{:S(2)}, u32[]{:S(2)}) collective-permute-start(f32[2,16,16]{1,2,0:T(8,128)S(1)} %get-tuple-element.18), channel_id=1, source_target_pairs={{0,4},{2,6},{4,0},{6,2},{1,5},{3,7},{5,1},{7,3},{8,12},{10,14},{12... | collective-permute-start | bytes 6152 | tf_op jit(solution)/shard_map/ppermute | solution.py:14
  32.9 23.7 %collective-permute-start = (f32[2,16,16]{1,2,0:T(8,128)S(1)}, f32[2,16,16]{1,2,0:T(8,128)S(1)}, u32[]{:S(2)}, u32[]{:S(2)}) collective-permute-start(f32[2,16,16]{1,2,0:T(8,128)S(1)} %get-tuple-element.18), channel_id=1, source_target_pairs={{0,2},{2,4},{4,6},{6,0},{1,3},{3,5},{5,7},{7,1},{8,10},{10,12},{12... | collective-permute-start | bytes 6152 | tf_op jit(solution)/shard_map/ppermute | solution.py:14
  54.6 21.7 %collective-permute-start.3 = (bf16[2,2,16,2048]{3,2,1,0:T(8,128)(2,1)S(1)}, bf16[2,2,16,2048]{3,2,1,0:T(8,128)(2,1)S(1)}, u32[]{:S(2)}, u32[]{:S(2)}) collective-permute-start(bf16[2,2,16,2048]{3,2,1,0:T(8,128)(2,1)S(1)} %get-tuple-element.16), channel_id=1, source_target_pairs={{0,2},{2,4},{4,6},{6,0},{1,3},{3,5},{5,7},{7,1},{8,10},{10,12},{12... | collective-permute-start | bytes 786440 | tf_op jit(solution)/shard_map/ppermute | solution.py:14
  83.0 17.9 %copy-start = (bf16[1,512,2,384]{3,2,1,0:T(2,128)(2,1)S(1)}, bf16[1,512,2,384]{3,2,1,0:T(2,128)(2,1)}, u32[]{:S(2)}) copy-start(bf16[1,512,2,384]{3,2,1,0:T(2,128)(2,1)} %param.12) | copy-start | bytes 2359300
  83.0 18.0 %copy-start.2 = (bf16[1,512,384]{2,1,0:T(8,128)(2,1)S(1)}, bf16[1,512,384]{2,1,0:T(8,128)(2,1)}, u32[]{:S(2)}) copy-start(bf16[1,512,384]{2,1,0:T(8,128)(2,1)} %param.13) | copy-start | bytes 1179652
  83.0 64.9 %all-to-all-start = ((bf16[32,32,2048]{2,1,0:T(8,128)(2,1)}), bf16[32,32,2048]{2,1,0:T(8,128)(2,1)}, u32[]{:S(2)}, u32[]{:S(2)}) async-start(bf16[32,32,2048]{2,1,0:T(8,128)(2,1)} %pad_maximum_fusion), calls=%async_computation | async-start | bytes 8388608 | tf_op jit(solution)/shard_map/all_to_all | solution.py:68
  150.4 106.4 %all-to-all-start.1 = ((bf16[4,512,1152]{2,1,0:T(8,128)(2,1)}), bf16[4,512,1152]{2,1,0:T(8,128)(2,1)}, u32[]{:S(2)}, u32[]{:S(2)}) async-start(bf16[4,512,1152]{2,1,0:T(8,128)(2,1)} %stack.68), calls=%async_computation.1 | async-start | bytes 9437184 | tf_op jit(solution)/shard_map/all_to_all | solution.py:40
  260.5 2.9 copy-start.1
  272.5 16.2 %copy-start.3 = (s32[64]{0:T(128)S(1)}, s32[64]{0:T(128)}, u32[]{:S(2)}) copy-start(s32[64]{0:T(128)} %param.11) | copy-start | bytes 772
  272.5 81.2 %all-to-all-start.2 = ((bf16[32,32,2048]{2,1,0:T(8,128)(2,1)}), bf16[32,32,2048]{2,1,0:T(8,128)(2,1)}, u32[]{:S(2)}, u32[]{:S(2)}) async-start(bf16[32,32,2048]{2,1,0:T(8,128)(2,1)} %pad_maximum_fusion.1), calls=%async_computation.2 | async-start | bytes 8388608 | tf_op jit(solution)/shard_map/all_to_all | solution.py:86
  281.9 54.5 %collective-permute-start.10 = (bf16[1,512,384]{2,1,0:T(8,128)(2,1)S(1)}, bf16[1,512,384]{2,1,0:T(8,128)(2,1)S(1)}, u32[]{:S(2)}, u32[]{:S(2)}) collective-permute-start(bf16[1,512,384]{2,1,0:T(8,128)(2,1)S(1)} %copy-done.2), channel_id=1, source_target_pairs={{0,64},{32,96},{64,0},{96,32},{1,65},{33,97},{65,1},{97,33},{2,66}... | collective-permute-start | bytes 1179656 | tf_op jit(solution)/shard_map/ppermute | solution.py:31
  284.1 92.3 %collective-permute-start.9 = (bf16[1,512,2,384]{3,2,1,0:T(2,128)(2,1)S(1)}, bf16[1,512,2,384]{3,2,1,0:T(2,128)(2,1)S(1)}, u32[]{:S(2)}, u32[]{:S(2)}) collective-permute-start(bf16[1,512,2,384]{3,2,1,0:T(2,128)(2,1)S(1)} %copy-done), channel_id=1, source_target_pairs={{0,64},{32,96},{64,0},{96,32},{1,65},{33,97},{65,1},{97,33},{2,66}... | collective-permute-start | bytes 2359304 | tf_op jit(solution)/shard_map/ppermute | solution.py:30
  360.6 22.1 %collective-permute-start.8 = (bf16[2,2,16,2048]{3,2,1,0:T(8,128)(2,1)S(1)}, bf16[2,2,16,2048]{3,2,1,0:T(8,128)(2,1)S(1)}, u32[]{:S(2)}, u32[]{:S(2)}) collective-permute-start(bf16[2,2,16,2048]{3,2,1,0:T(8,128)(2,1)S(1)} %get-tuple-element.11), channel_id=1, source_target_pairs={{0,2},{2,4},{4,6},{6,0},{1,3},{3,5},{5,7},{7,1},{8,10},{10,12},{12... | collective-permute-start | bytes 786440 | tf_op jit(solution)/shard_map/ppermute | solution.py:14
  362.5 30.2 %collective-permute-start.7 = (bf16[2,2,16,2048]{3,2,1,0:T(8,128)(2,1)S(1)}, bf16[2,2,16,2048]{3,2,1,0:T(8,128)(2,1)S(1)}, u32[]{:S(2)}, u32[]{:S(2)}) collective-permute-start(bf16[2,2,16,2048]{3,2,1,0:T(8,128)(2,1)S(1)} %get-tuple-element.12), channel_id=1, source_target_pairs={{0,4},{2,6},{4,0},{6,2},{1,5},{3,7},{5,1},{7,3},{8,12},{10,14},{12... | collective-permute-start | bytes 786440 | tf_op jit(solution)/shard_map/ppermute | solution.py:14
  372.0 50.0 %collective-permute-start.6 = (bf16[2,2,16,2048]{3,2,1,0:T(8,128)(2,1)S(1)}, bf16[2,2,16,2048]{3,2,1,0:T(8,128)(2,1)S(1)}, u32[]{:S(2)}, u32[]{:S(2)}) collective-permute-start(bf16[2,2,16,2048]{3,2,1,0:T(8,128)(2,1)S(1)} %get-tuple-element.10), channel_id=1, source_target_pairs={{0,6},{2,0},{4,2},{6,4},{1,7},{3,1},{5,3},{7,5},{8,14},{10,8},{12,... | collective-permute-start | bytes 786440 | tf_op jit(solution)/shard_map/ppermute | solution.py:14
